TPU v7x, 32 devices: a whole 2x2x4 slice. The times are simulated.
32 devices in a mesh: groups: 2 (over y), block: 4 (over x, core), tensor: 4 (over z).
Axes of the slice: x: 2, y: 2, z: 4, core: 2. Of those that a mesh axis runs over, the one named last changes fastest.
Arguments:
- tokens: bfloat16 [4096, 5120], P(('groups', 'block', 'tensor')), parts along dimension 0, may hold values from -20 to 20
- mod_shift: float32 [5120], replicated, may hold values from -3 to 3
- mod_scale: float32 [5120], replicated, may hold values from -0.5 to 0.5
- w_qkv: bfloat16 [3, 5120, 1024], P(None, 'block', 'tensor'), may hold values from -1 to 1
- tile_list: int32 [8, 4, 5], P(('groups', 'block')), parts along dimension 0, may hold values from 0 to 7, as said below
- tile_count: int32 [8, 4], P(('groups', 'block')), parts along dimension 0, may hold values from 2 to 5, as said below
Outputs:
- attended: bfloat16 [4096, 1024], P(('groups', 'block'), 'tensor'), parts along dimension 0
There are 2 independent parts, one for each index of `groups`. A program takes and returns all parts, laid end to end along the dimension named above; an argument that names none is the same for every part. Nothing has to cross between parts.
Inputs may be any that keep to these rules, and one draw needn't show every extreme that they name: `tile_list`: within the first tile_count[c, t] slots the entries are distinct, the first is the query tile itself (2 + t), and none names a tile outside the slab; blocks at scene cuts name no tile of the block across the cut. Later slots hold indices in range and are not read. `tile_count`: the first query tile of every block reads 5 slots.
All inputs are finite; a program needn't handle non-finite values.
Results may differ from a plain program's by a relative error of at most 0.0087.
Values may be sent and summed in bfloat16 or wider, within the bound.
A program may use at most 64 MiB of HBM per device.

v0:
```python
import jax
import jax.numpy as jnp
from jax import lax
from jax.sharding import PartitionSpec as P

HEAD_DIM = 128
TILE = 128
BT = 2


epsilon = 1e-06


def with_halo(x, sides, width):
    for axis, dim in sides:
        count, length = (lax.axis_size(axis), x.shape[dim])
        up = [(i, (i + 1) % count) for i in range(count - 1)]
        down = [(j, i) for i, j in up]
        last = lax.slice_in_dim(x, length - width, length, axis=dim)
        first = lax.slice_in_dim(x, 0, width, axis=dim)
        before = lax.ppermute(last, axis, up)
        after = lax.ppermute(first, axis, down)
        x = jnp.concatenate([before, x, after], axis=dim)
    return x


def attend(queries, key_rows, value_rows, chosen_list, chosen_count):
    head_count = queries.shape[1] // HEAD_DIM
    local_tiles = queries.shape[0] // TILE
    all_tiles = key_rows.shape[0] // TILE
    slot_count = chosen_list.shape[1]
    shaped_queries = queries.reshape(local_tiles, TILE, head_count, HEAD_DIM)
    key_tiles = key_rows.reshape(all_tiles, TILE, head_count, HEAD_DIM)[chosen_list]
    value_tiles = value_rows.reshape(all_tiles, TILE, head_count, HEAD_DIM)[chosen_list]
    scores = jnp.einsum(
        "pthd,pkshd->phtks", shaped_queries, key_tiles, preferred_element_type=jnp.float32
    )
    scores = scores * HEAD_DIM ** (-0.5)
    live_slot = jnp.arange(slot_count, dtype=jnp.int32)[None, :] < chosen_count[:, None]
    scores = jnp.where(live_slot[:, None, None, :, None], scores, jnp.float32(-1e30))
    highest = jnp.max(scores, axis=(3, 4), keepdims=True)
    exponent = jnp.exp(scores - highest)
    denominator = jnp.sum(exponent, axis=(3, 4), keepdims=True)
    attn_weights = (exponent / denominator).astype(jnp.bfloat16)
    mixed = jnp.einsum(
        "phtks,pkshd->pthd", attn_weights, value_tiles, preferred_element_type=jnp.float32
    )
    return mixed.astype(jnp.bfloat16).reshape(local_tiles * TILE, head_count * HEAD_DIM)


def shards(tokens, mod_shift, mod_scale, w_qkv, tile_list, tile_count):
    values_in = tokens.astype(jnp.float32)
    row_mean = jnp.mean(values_in, axis=1, keepdims=True)
    centred = values_in - row_mean
    row_var = jnp.mean(centred * centred, axis=1, keepdims=True)
    normed = (centred * lax.rsqrt(row_var + epsilon) * (1.0 + mod_scale) + mod_shift).astype(
        jnp.bfloat16
    )
    gathered = lax.all_gather(normed, "tensor", axis=0, tiled=True)
    projected = jnp.einsum(
        "td,ide->ite",
        gathered,
        lax.all_gather(w_qkv, "block", axis=1, tiled=True),
        preferred_element_type=jnp.float32,
    )
    projected = projected.astype(jnp.bfloat16)
    queries = projected[0]
    key_value = projected[1:3]
    extended = with_halo(key_value, (("block", 1),), BT * TILE)
    return attend(queries, extended[0], extended[1], tile_list[0], tile_count[0])


def solution(mesh):
    return jax.shard_map(
        shards,
        mesh=mesh,
        in_specs=(
            P(("groups", "block", "tensor"), None),
            P(),
            P(),
            P(None, "block", "tensor"),
            P(("groups", "block"), None, None),
            P(("groups", "block"), None),
        ),
        out_specs=P(("groups", "block"), "tensor"),
        check_vma=False,
    )
```

profile of v0, /device:TPU:1, one launch (start us, length us, event | category | flops | bytes accessed | tf_op | source)
XLA Modules:
  0.0 203.6 jit_solution(6897856617463823574)
XLA Ops:
  6.5 1.7 convert_reduce_fusion
  8.2 1.8 fusion.4
  10.1 0.0 copy-start.3
  10.1 1.7 fusion.7
  11.8 0.0 all-gather.3.cloned.1.call-update
  11.8 0.0 all-gather.5.cloned.1.call-start
  11.9 0.7 all-gather.5.cloned.1.call-update
  12.6 0.1 reshape.73
  12.7 99.6 %all-gather.3.cloned.1.call-done = bf16[512,5120]{1,0:T(8,128)(2,1)} async-done(((bf16[128,5120]{1,0:T(8,128)(2,1)}), bf16[512,5120]{1,0:T(8,128)(2,1)}) %all-gather.3.cloned.1.call-update) | async-done | bytes 5242896 | tf_op jit(solution)/shard_map/all_gather | solution.py:59
  112.3 55.5 %all-gather.5.cloned.1.call-done = bf16[3,5120,256]{2,1,0:T(8,128)(2,1)} async-done(((bf16[3,1280,256]{2,1,0:T(8,128)(2,1)}), bf16[3,5120,256]{2,1,0:T(8,128)(2,1)}) %all-gather.5.cloned.1.call-update) | async-done | bytes 7864336 | tf_op jit(solution)/shard_map/all_gather | solution.py:63
  167.8 9.0 %fusion.16 = bf16[3,512,256]{2,1,0:T(8,128)(2,1)S(1)} fusion(bf16[3,5120,256]{2,1,0:T(8,128)(2,1)} %all-gather.5.cloned.1.call-done, bf16[512,5120]{1,0:T(8,128)(2,1)} %all-gather.3.cloned.1.call-done), kind=kOutput, calls=%fused_computation.21 | convolution fusion | flops 4026925056 | bytes 13893632 | tf_op jit(solution)/shard_map/td,ide->ite/dot_general | solution.py:60
  176.9 2.1 %collective-permute-start = (bf16[2,256,256]{2,1,0:T(8,128)(2,1)S(1)}, bf16[2,256,256]{2,1,0:T(8,128)(2,1)S(1)}, u32[]{:S(2)}, u32[]{:S(2)}) collective-permute-start(bf16[2,256,256]{2,1,0:T(8,128)(2,1)S(1)} %get-tuple-element.7), channel_id=1, source_target_pairs={{0,4},{4,8},{8,12},{1,5},{5,9},{9,13},{2,6},{6,10},{10,14},{3,7},{... | collective-permute-start | bytes 786440 | tf_op jit(solution)/shard_map/ppermute | solution.py:21
  179.0 2.3 %collective-permute-start.1 = (bf16[2,256,256]{2,1,0:T(8,128)(2,1)S(1)}, bf16[2,256,256]{2,1,0:T(8,128)(2,1)S(1)}, u32[]{:S(2)}, u32[]{:S(2)}) collective-permute-start(bf16[2,256,256]{2,1,0:T(8,128)(2,1)S(1)} %get-tuple-element.8), channel_id=1, source_target_pairs={{4,0},{8,4},{12,8},{5,1},{9,5},{13,9},{6,2},{10,6},{14,10},{7,3},{... | collective-permute-start | bytes 786440 | tf_op jit(solution)/shard_map/ppermute | solution.py:22
  181.2 0.1 iota_compare_fusion
  181.4 0.1 reshape_squeeze.10
  181.5 0.8 collective-permute-done
  182.3 4.4 %collective-permute-done.1 = bf16[2,256,256]{2,1,0:T(8,128)(2,1)S(1)} collective-permute-done((bf16[2,256,256]{2,1,0:T(8,128)(2,1)S(1)}, bf16[2,256,256]{2,1,0:T(8,128)(2,1)S(1)}, u32[]{:S(2)}, u32[]{:S(2)}) %collective-permute-start.1) | collective-permute-done | bytes 262176 | tf_op jit(solution)/shard_map/ppermute | solution.py:22
  186.6 0.1 pad_maximum_fusion
  186.7 0.1 fusion.32
  186.8 0.1 reshape_squeeze.11
  186.9 0.1 copy.15
  187.0 0.8 gather_fusion.1
  187.8 0.1 copy.17
  188.0 0.5 fusion.28
  188.5 0.4 fusion.8
  188.9 0.6 fusion.9
  189.5 0.9 reshape_squeeze.9
  190.4 1.1 copy.14
  191.6 1.9 gather_fusion
  193.4 2.4 %fusion.25 = bf16[4,128,2,128]{1,3,2,0:T(8,128)(2,1)S(1)} fusion(f32[4,2,128,5,128]{2,4,3,1,0:T(8,128)S(1)} %bitcast.38, f32[4,2,128]{2,1,0:T(2,128)S(1)} %fusion.9, f32[4,2,128]{2,1,0:T(2,128)S(1)} %fusion.8, pred[4,5]{1,0:T(4,128)(4,1)S(1)} %iota_compare_fusion, bf16[4,5,128,2,128]{4,2,3,1,0:T(8,128)(2,1)} %bitcast.41), kind=kOutput, calls=%fused_computation.24 | convolution fusion | flops 171180032 | bytes 4202516 | tf_op jit(solution)/shard_map/phtks,pkshd->pthd/dot_general | solution.py:45
  195.8 0.2 copy.20
  196.0 0.7 copy.37
  (18 shorter events, 0.1 us)
Async XLA Ops:
  6.5 3.6 %copy-start = (bf16[128,5120]{1,0:T(8,128)(2,1)S(1)}, bf16[128,5120]{1,0:T(8,128)(2,1)}, u32[]{:S(2)}) copy-start(bf16[128,5120]{1,0:T(8,128)(2,1)} %param.6) | copy-start | bytes 3932164
  6.5 3.5 %copy-start.2 = (f32[5120]{0:T(1024)S(1)}, f32[5120]{0:T(1024)}, u32[]{:S(2)}) copy-start(f32[5120]{0:T(1024)} %param.8) | copy-start | bytes 61444
  6.5 3.6 %copy-start.1 = (f32[5120]{0:T(1024)S(1)}, f32[5120]{0:T(1024)}, u32[]{:S(2)}) copy-start(f32[5120]{0:T(1024)} %param.7) | copy-start | bytes 61444
  6.5 105.7 %all-gather.3.cloned.1.call-start = ((), (), s32[]{:S(2)}) async-start(), calls=%async_computation | async-start | bytes 6553600 | tf_op jit(solution)/shard_map/all_gather | solution.py:59
  10.1 2.4 %copy-start.3 = (s32[1,4,5]{2,1,0:T(4,128)S(1)}, s32[1,4,5]{2,1,0:T(4,128)}, u32[]{:S(2)}) copy-start(s32[1,4,5]{2,1,0:T(4,128)} %param.10) | copy-start | bytes 244
  11.8 156.0 %all-gather.5.cloned.1.call-start = ((), (), s32[]{:S(2)}) async-start(), calls=%async_computation.1 | async-start | bytes 9830400 | tf_op jit(solution)/shard_map/all_gather | solution.py:63
  12.7 168.6 %copy-start.4 = (s32[1,4]{1,0:T(1,128)S(1)}, s32[1,4]{1,0:T(1,128)}, u32[]{:S(2)}) copy-start(s32[1,4]{1,0:T(1,128)} %param.11) | copy-start | bytes 52
  176.9 5.4 %collective-permute-start = (bf16[2,256,256]{2,1,0:T(8,128)(2,1)S(1)}, bf16[2,256,256]{2,1,0:T(8,128)(2,1)S(1)}, u32[]{:S(2)}, u32[]{:S(2)}) collective-permute-start(bf16[2,256,256]{2,1,0:T(8,128)(2,1)S(1)} %get-tuple-element.7), channel_id=1, source_target_pairs={{0,4},{4,8},{8,12},{1,5},{5,9},{9,13},{2,6},{6,10},{10,14},{3,7},{... | collective-permute-start | bytes 786440 | tf_op jit(solution)/shard_map/ppermute | solution.py:21
  179.0 7.7 %collective-permute-start.1 = (bf16[2,256,256]{2,1,0:T(8,128)(2,1)S(1)}, bf16[2,256,256]{2,1,0:T(8,128)(2,1)S(1)}, u32[]{:S(2)}, u32[]{:S(2)}) collective-permute-start(bf16[2,256,256]{2,1,0:T(8,128)(2,1)S(1)} %get-tuple-element.8), channel_id=1, source_target_pairs={{4,0},{8,4},{12,8},{5,1},{9,5},{13,9},{6,2},{10,6},{14,10},{7,3},{... | collective-permute-start | bytes 786440 | tf_op jit(solution)/shard_map/ppermute | solution.py:22
Sparse Core Ops, SparseCore 0:
  11.9 100.2 all-gather.2
  113.8 53.9 all-gather.4
where the time goes:
time: 204 us
  waiting for transfers between devices  161 us (79%)
  between operations  13.6 us (7%)
  matrix products  11.9 us (6%)
  other arithmetic  6.35 us (3%)
  local copies, waits for them, and re-layouts  6.3 us (3%)
  starting transfers between devices  4.38 us (2%)
    all_gather x1, waiting for transfers between devices, shards(): gathered = lax.all_gather(normed, 'tensor', axis=0, tiled=True)  99.6 us
    all_gather x1, waiting for transfers between devices, shards(): lax.all_gather(w_qkv, 'block', axis=1, tiled=True)  55.5 us
    dot_general x1, matrix products, shards(): jnp.einsum('td,ide->ite', gathered, lax.all_gather(w_qkv, 'block', axis=1...  9.02 us
    ppermute x1, waiting for transfers between devices, with_halo(): after = lax.ppermute(first, axis, down)  4.4 us
  transfers between devices with their start and end apart: 4, of which 4 were waited for; matrix products, arithmetic and copies ran while one was open for 0% of the time, Pallas kernels for 0%

commit v1 on v0

v1 whole, which is shorter than its diff:
```python
import functools

import jax
import jax.numpy as jnp
from jax import lax
from jax.experimental import pallas as pl
from jax.experimental.pallas import tpu as pltpu
from jax.sharding import PartitionSpec as P

HEAD_DIM = 128
TILE = 128
BT = 2
MARGIN = BT * TILE
CHUNK = 32
MESH = pl.DeviceIdType.MESH

epsilon = 1e-06


def project_kernel(
    nb, nt, tokens_ref, shift_ref, scale_ref, w_ref, q_ref, kv_ref,
    xg, wfull, qkvx, up_s, up_r, dn_s, dn_r, wx_s, wx_r, wp_s, wp_r, wl_s, hu_s, hu_r, hd_s, hd_r,
):
    g = lax.axis_index("groups")
    b = lax.axis_index("block")
    t = lax.axis_index("tensor")
    rows, _ = tokens_ref.shape
    kb = w_ref.shape[1]
    nc = rows // CHUNK
    total = rows * nt
    chips = nb // 2
    chip = b // 2
    core = b % 2
    partner = (g, chip * 2 + (1 - core), t)

    barrier = pltpu.get_barrier_semaphore()
    for j in range(1, nb):
        pl.semaphore_signal(barrier, inc=1, device_id=(g, (b + j) % nb, t), device_id_type=MESH)

    @pl.when(t > 0)
    def _():
        pl.semaphore_signal(barrier, inc=1, device_id=(g, b, t - 1), device_id_type=MESH)

    @pl.when(t < nt - 1)
    def _():
        pl.semaphore_signal(barrier, inc=1, device_id=(g, b, t + 1), device_id_type=MESH)

    ends = jnp.where(t == 0, 1, 0) + jnp.where(t == nt - 1, 1, 0)
    pl.semaphore_wait(barrier, nb + 1 - ends)

    def remote(src, dst, s, r, device):
        return pltpu.make_async_remote_copy(
            src_ref=src, dst_ref=dst, send_sem=s, recv_sem=r, device_id=device, device_id_type=MESH
        )

    def w_slab(owner, i):
        return wfull.at[i, pl.ds(pl.multiple_of(owner * kb, 16), kb)]

    def w_cross(j, i, owner, device):
        return remote(w_ref.at[i], w_slab(owner, i), wx_s.at[j, i], wx_r.at[j, i], device)

    def w_pair(j, i, src, owner):
        return remote(src, w_slab(owner, i), wp_s.at[j, i], wp_r.at[j, i], partner)

    for i in range(3):
        for j in range(1, chips):
            w_cross(j, i, b, (g, ((chip + j) % chips) * 2 + core, t)).start()
        w_pair(0, i, w_ref.at[i], b).start()
        pltpu.make_async_copy(w_ref.at[i], w_slab(b, i), wl_s.at[i]).start()

    def x_slab(o, c):
        return xg.at[pl.ds(pl.multiple_of(o * rows + c * CHUNK, 16), CHUNK)]

    def up(s, c):
        slab = x_slab(t - s, c)
        return remote(slab, slab, up_s.at[s, c], up_r.at[s, c], (g, b, t + 1))

    def down(s, c):
        slab = x_slab(t + s, c)
        return remote(slab, slab, dn_s.at[s, c], dn_r.at[s, c], (g, b, t - 1))

    def from_left(s, c):
        slab = x_slab(t - s, c)
        return remote(slab, slab, up_s.at[s - 1, c], up_r.at[s - 1, c], (g, b, t + 1))

    def from_right(s, c):
        slab = x_slab(t + s, c)
        return remote(slab, slab, dn_s.at[s - 1, c], dn_r.at[s - 1, c], (g, b, t - 1))

    gain = 1.0 + scale_ref[...]

    def norm(c, carry):
        x = tokens_ref[pl.ds(pl.multiple_of(c * CHUNK, 16), CHUNK), :].astype(jnp.float32)
        mean = jnp.mean(x, axis=1, keepdims=True)
        x = x - mean
        var = jnp.mean(x * x, axis=1, keepdims=True)
        y = x * lax.rsqrt(var + epsilon) * gain + shift_ref[...]
        xg[pl.ds(pl.multiple_of(t * rows + c * CHUNK, 16), CHUNK), :] = y.astype(jnp.bfloat16)

        @pl.when(t < nt - 1)
        def _():
            up(0, c).start()

        @pl.when(t > 0)
        def _():
            down(0, c).start()

        return carry

    lax.fori_loop(0, nc, norm, 0)

    zeros = jnp.zeros((2, MARGIN, qkvx.shape[2]), qkvx.dtype)

    @pl.when(b == 0)
    def _():
        qkvx[1:3, 0:MARGIN, :] = zeros

    @pl.when(b == nb - 1)
    def _():
        qkvx[1:3, MARGIN + total : 2 * MARGIN + total, :] = zeros

    def relay(s):
        def body(c, carry):
            @pl.when(t - s >= 0)
            def _():
                from_left(s, c).wait_recv()

                @pl.when(t < nt - 1)
                def _():
                    up(s, c).start()

            @pl.when(t + s < nt)
            def _():
                from_right(s, c).wait_recv()

                @pl.when(t > 0)
                def _():
                    down(s, c).start()

            return carry

        lax.fori_loop(0, nc, body, 0)

    def halo_up(o):
        return remote(
            qkvx.at[1:3, pl.ds(pl.multiple_of(MARGIN + o * rows, 16), rows)],
            qkvx.at[1:3, pl.ds(pl.multiple_of(o * rows - (total - MARGIN), 16), rows)],
            hu_s.at[o], hu_r.at[o], (g, b + 1, t),
        )

    def halo_down(o):
        return remote(
            qkvx.at[1:3, pl.ds(pl.multiple_of(MARGIN + o * rows, 16), rows)],
            qkvx.at[1:3, pl.ds(pl.multiple_of(MARGIN + total + o * rows, 16), rows)],
            hd_s.at[o], hd_r.at[o], (g, b - 1, t),
        )

    def project(o):
        x = xg[pl.ds(pl.multiple_of(o * rows, 16), rows), :]

        def one(i, carry):
            y = jnp.dot(x, wfull[i], preferred_element_type=jnp.float32)
            qkvx[i, pl.ds(pl.multiple_of(MARGIN + o * rows, 16), rows), :] = y.astype(jnp.bfloat16)
            return carry

        lax.fori_loop(0, 3, one, 0)

        @pl.when(jnp.logical_and(o * rows >= total - MARGIN, b < nb - 1))
        def _():
            halo_up(o).start()

        @pl.when(jnp.logical_and(o * rows < MARGIN, b > 0))
        def _():
            halo_down(o).start()

    relay(1)

    for i in range(3):
        for j in range(1, chips):
            owner = ((chip - j + chips) % chips) * 2 + core
            w_cross(j, i, owner, partner).wait_recv()
            w_pair(j, i, w_slab(owner, i), owner).start()
    for i in range(3):
        pltpu.make_async_copy(w_ref.at[i], w_slab(b, i), wl_s.at[i]).wait()
        for j in range(chips):
            owner = ((chip - j + chips) % chips) * 2 + (1 - core)
            w_pair(j, i, w_slab(owner, i), owner).wait_recv()

    project(t)

    def step(s, carry):
        @pl.when(s > 1)
        def _():
            relay(s)

        def side(d, carry):
            o = t + s * (2 * d - 1)

            @pl.when(jnp.logical_and(o >= 0, o < nt))
            def _():
                project(o)

            return carry

        lax.fori_loop(0, 2, side, 0)
        return carry

    lax.fori_loop(1, nt, step, 0)

    def drain(s, carry):
        def body(c, carry):
            @pl.when(jnp.logical_and(t - s >= 0, t < nt - 1))
            def _():
                up(s, c).wait_send()

            @pl.when(jnp.logical_and(t + s < nt, t > 0))
            def _():
                down(s, c).wait_send()

            return carry

        return lax.fori_loop(0, nc, body, carry)

    lax.fori_loop(0, nt, drain, 0)
    for i in range(3):
        for j in range(1, chips):
            w_cross(j, i, b, partner).wait_send()
        for j in range(chips):
            w_pair(j, i, w_ref.at[i], b).wait_send()

    q_ref[...] = qkvx[0, MARGIN : MARGIN + total, :]

    def halo_wait(o, carry):
        @pl.when(o * rows >= total - MARGIN)
        def _():
            @pl.when(b < nb - 1)
            def _():
                halo_up(o).wait_send()

            @pl.when(b > 0)
            def _():
                halo_up(o).wait_recv()

        @pl.when(o * rows < MARGIN)
        def _():
            @pl.when(b > 0)
            def _():
                halo_down(o).wait_send()

            @pl.when(b < nb - 1)
            def _():
                halo_down(o).wait_recv()

        return carry

    lax.fori_loop(0, nt, halo_wait, 0)
    kv_ref[...] = qkvx[1:3]


def attend_kernel(list_ref, count_ref, q_ref, kv_ref, out_ref):
    tiles = q_ref.shape[0] // TILE
    heads = q_ref.shape[1] // HEAD_DIM
    slots = list_ref.shape[2]
    for p in range(tiles):
        count = count_ref[0, p]
        starts = [pl.multiple_of(list_ref[0, p, s] * TILE, TILE) for s in range(slots)]
        for h in range(heads):
            cols = slice(h * HEAD_DIM, (h + 1) * HEAD_DIM)
            q = q_ref[p * TILE : (p + 1) * TILE, cols]
            keys = jnp.concatenate([kv_ref[0, pl.ds(a, TILE), cols] for a in starts], axis=0)
            vals = jnp.concatenate([kv_ref[1, pl.ds(a, TILE), cols] for a in starts], axis=0)
            scores = lax.dot_general(
                q, keys, (((1,), (1,)), ((), ())), preferred_element_type=jnp.float32
            ) * HEAD_DIM ** (-0.5)
            slot = lax.broadcasted_iota(jnp.int32, scores.shape, 1) // TILE
            scores = jnp.where(slot < count, scores, jnp.float32(-1e30))
            e = jnp.exp(scores - jnp.max(scores, axis=1, keepdims=True))
            weights = (e / jnp.sum(e, axis=1, keepdims=True)).astype(jnp.bfloat16)
            mixed = jnp.dot(weights, vals, preferred_element_type=jnp.float32)
            out_ref[p * TILE : (p + 1) * TILE, cols] = mixed.astype(jnp.bfloat16)


def shards(nb, nt, tokens, mod_shift, mod_scale, w_qkv, tile_list, tile_count):
    rows, d = tokens.shape
    width = w_qkv.shape[2]
    total = rows * nt
    nc = rows // CHUNK
    chips = nb // 2
    vmem = pl.BlockSpec(memory_space=pltpu.VMEM)
    smem = pl.BlockSpec(memory_space=pltpu.SMEM)
    dma = pltpu.SemaphoreType.DMA
    bf16 = jnp.bfloat16
    q, kv = pl.pallas_call(
        functools.partial(project_kernel, nb, nt),
        out_shape=(
            jax.ShapeDtypeStruct((total, width), bf16),
            jax.ShapeDtypeStruct((2, total + 2 * MARGIN, width), bf16),
        ),
        in_specs=[vmem, vmem, vmem, pl.BlockSpec(memory_space=pl.ANY)],
        out_specs=(vmem, vmem),
        scratch_shapes=[
            pltpu.VMEM((total, d), bf16),
            pltpu.VMEM((3, d, width), bf16),
            pltpu.VMEM((3, total + 2 * MARGIN, width), bf16),
            dma((nt, nc)), dma((nt, nc)), dma((nt, nc)), dma((nt, nc)),
            dma((chips, 3)), dma((chips, 3)), dma((chips, 3)), dma((chips, 3)), dma((3,)),
            dma((nt,)), dma((nt,)), dma((nt,)), dma((nt,)),
        ],
        compiler_params=pltpu.CompilerParams(
            collective_id=0, has_side_effects=True, vmem_limit_bytes=40 * 2**20
        ),
    )(tokens, mod_shift.reshape(1, d), mod_scale.reshape(1, d), w_qkv)
    return pl.pallas_call(
        attend_kernel,
        out_shape=jax.ShapeDtypeStruct((total, width), bf16),
        in_specs=[smem, smem, vmem, vmem],
        out_specs=vmem,
        compiler_params=pltpu.CompilerParams(vmem_limit_bytes=32 * 2**20),
    )(tile_list, tile_count, q, kv)


def solution(mesh):
    return jax.shard_map(
        functools.partial(shards, mesh.shape["block"], mesh.shape["tensor"]),
        mesh=mesh,
        in_specs=(
            P(("groups", "block", "tensor"), None),
            P(),
            P(),
            P(None, "block", "tensor"),
            P(("groups", "block"), None, None),
            P(("groups", "block"), None),
        ),
        out_specs=P(("groups", "block"), "tensor"),
        check_vma=False,
    )
```

time: 204 us -> 104 us (0.51)
  waiting for transfers between devices: 161 us -> 0 us
  Pallas kernels: 0 us -> 99 us
  between operations: 13.6 us -> 0.03 us
  matrix products: 11.9 us -> 0 us
  other arithmetic: 6.35 us -> 0 us
  starting transfers between devices: 4.38 us -> 0 us
    all_gather x2 -> x0, waiting for transfers between devices: 155 us -> none  [the longest x1 99.6 us: shards(): gathered = lax.all_gather(normed, 'tensor', axis=0, tiled=True)]
    pallas_call x0 -> x2, Pallas kernels: none -> 99 us  [the longest x1 94.5 us: shards(): pl.pallas_call(functools.partial(project_kernel, nb, nt), out_shape=(jax....]
    dot_general x2 -> x0, matrix products: 11.4 us -> none  [the longest x1 9.02 us: shards(): jnp.einsum('td,ide->ite', gathered, lax.all_gather(w_qkv, 'block', axis=1...]
    ppermute x2 -> x0, waiting for transfers between devices: 5.19 us -> none  [the longest x1 4.4 us: with_halo(): after = lax.ppermute(first, axis, down)]
    ppermute x2 -> x0, starting transfers between devices: 4.34 us -> none  [the longest x1 2.26 us: with_halo(): after = lax.ppermute(first, axis, down)]
    reduce_sum x3 -> x0, other arithmetic: 4.12 us -> none  [the longest x1 1.82 us: shards(): row_var = jnp.mean(centred * centred, axis=1, keepdims=True)]
    unnamed x11 -> x12, local copies, waits for them, and re-layouts: 0.76 us -> 4.35 us
    gather x3 -> x0, local copies, waits for them, and re-layouts: 2.79 us -> none  [the longest x1 1.85 us: attend(): value_rows.reshape(all_tiles, TILE, head_count, HEAD_DIM)[chosen_list]]
  transfers between devices with their start and end apart: 4 -> 0, of which waited for: 4 -> 0; matrix products, arithmetic and copies ran while one was open for 0% -> 0% of each run, Pallas kernels for 0% -> 0%
where the time goes in v1:
time: 104 us; the launch traced here: 103 us
  Pallas kernels  99 us (95%)
  local copies, waits for them, and re-layouts  4.35 us (4%)
    pallas_call x1, Pallas kernels, shards(): pl.pallas_call(functools.partial(project_kernel, nb, nt), out_shape=(jax....  94.5 us
    pallas_call x1, Pallas kernels, shards(): pl.pallas_call(attend_kernel, out_shape=jax.ShapeDtypeStruct((total, widt...  4.58 us
    unnamed x12, local copies, waits for them, and re-layouts  4.35 us

profile of v1, /device:TPU:1, one launch (start us, length us, event | category | flops | bytes accessed | tf_op | source)
XLA Modules:
  0.0 103.4 jit_solution(3066782639394248083)
XLA Ops:
  0.0 0.0 copy-start.5
  0.0 0.0 copy-start.4
  0.0 0.0 copy-start
  0.0 1.6 %copy-done = bf16[3,1280,256]{2,1,0:T(8,128)(2,1)S(1)} copy-done((bf16[3,1280,256]{2,1,0:T(8,128)(2,1)S(1)}, bf16[3,1280,256]{2,1,0:T(8,128)(2,1)}, u32[]{:S(2)}) %copy-start) | copy-done | bytes 1966104
  1.6 0.0 copy-start.1
  1.6 1.3 %copy-done.1 = bf16[128,5120]{1,0:T(8,128)(2,1)S(1)} copy-done((bf16[128,5120]{1,0:T(8,128)(2,1)S(1)}, bf16[128,5120]{1,0:T(8,128)(2,1)}, u32[]{:S(2)}) %copy-start.1) | copy-done | bytes 1310744
  2.9 0.0 copy-start.2
  2.9 0.7 copy-done.2
  3.6 0.0 copy-start.3
  3.6 0.7 copy-done.3
  4.4 94.5 %shard_map.64 = (bf16[512,256]{1,0:T(8,128)(2,1)S(1)}, bf16[2,1024,256]{2,1,0:T(8,128)(2,1)S(1)}) custom-call(bf16[128,5120]{1,0:T(8,128)(2,1)S(1)} %copy-done.1, f32[1,5120]{1,0:T(1,128)S(1)} %bitcast.2, f32[1,5120]{1,0:T(1,128)S(1)} %bitcast.3, bf16[3,1280,256]{2,1,0:T(8,128)(2,1)S(1)} %copy-done), custom_call_target="tpu_custom_call" | custom-call | tf_op jit(solution)/shard_map/pallas_call | solution.py:293
  98.8 0.0 copy-done.5
  98.8 0.0 copy-done.4
  98.8 4.6 %shard_map.65 = bf16[512,256]{1,0:T(8,128)(2,1)} custom-call(s32[1,4,5]{2,1,0:T(4,128)S(1)} %copy-done.4, s32[1,4]{1,0:T(1,128)S(1)} %copy-done.5, bf16[512,256]{1,0:T(8,128)(2,1)S(1)} %get-tuple-element.7.q_ref, bf16[2,1024,256]{2,1,0:T(8,128)(2,1)S(1)} %get-tuple-element.8.kv_ref), custom_call_target="tpu_custom_call" | custom-call | tf_op jit(solution)/shard_map/pallas_call | solution.py:313
Async XLA Ops:
  0.0 98.8 %copy-start.5 = (s32[1,4]{1,0:T(1,128)S(1)}, s32[1,4]{1,0:T(1,128)}, u32[]{:S(2)}) copy-start(s32[1,4]{1,0:T(1,128)} %count_ref.1) | copy-start | bytes 52
  0.0 98.8 %copy-start.4 = (s32[1,4,5]{2,1,0:T(4,128)S(1)}, s32[1,4,5]{2,1,0:T(4,128)}, u32[]{:S(2)}) copy-start(s32[1,4,5]{2,1,0:T(4,128)} %list_ref.1) | copy-start | bytes 244
  0.0 1.6 %copy-start = (bf16[3,1280,256]{2,1,0:T(8,128)(2,1)S(1)}, bf16[3,1280,256]{2,1,0:T(8,128)(2,1)}, u32[]{:S(2)}) copy-start(bf16[3,1280,256]{2,1,0:T(8,128)(2,1)} %w_ref.1) | copy-start | bytes 5898244
  1.6 1.3 %copy-start.1 = (bf16[128,5120]{1,0:T(8,128)(2,1)S(1)}, bf16[128,5120]{1,0:T(8,128)(2,1)}, u32[]{:S(2)}) copy-start(bf16[128,5120]{1,0:T(8,128)(2,1)} %tokens_ref.1) | copy-start | bytes 3932164
  2.9 0.7 copy-start.2
  3.6 0.7 copy-start.3

commit v2 on v1

--- a/solution.py
+++ b/solution.py
@@ -18,9 +18,12 @@
 
 
 def project_kernel(
-    nb, nt, tokens_ref, shift_ref, scale_ref, w_ref, q_ref, kv_ref,
-    xg, wfull, qkvx, up_s, up_r, dn_s, dn_r, wx_s, wx_r, wp_s, wp_r, wl_s, hu_s, hu_r, hd_s, hd_r,
+    helped, nb, nt, tokens_hbm, shift_ref, scale_ref, w_ref, q_ref, kv_ref,
+    tokens_ref, xg, wfull, qkvx, wh, part_out, part_in, up_s, up_r, dn_s, dn_r, wx_s, wx_r, wp_s, wp_r, wl_s,
+    hu_s, hu_r, hd_s, hd_r, hz_s, hz_r, hy_s, hy_r, hp_s, hp_r, pt_s, pt_r, tk_s,
 ):
+    tokens_copy = pltpu.make_async_copy(tokens_hbm, tokens_ref, tk_s)
+    tokens_copy.start()
     g = lax.axis_index("groups")
     b = lax.axis_index("block")
     t = lax.axis_index("tensor")
@@ -32,6 +35,10 @@
     chip = b // 2
     core = b % 2
     partner = (g, chip * 2 + (1 - core), t)
+    lower = t < nt // 2
+    sgn = jnp.where(lower, -1, 1)
+    is_end = jnp.logical_or(t == 0, t == nt - 1)
+    kc = 2 * kb
 
     barrier = pltpu.get_barrier_semaphore()
     for j in range(1, nb):
@@ -45,8 +52,10 @@
     def _():
         pl.semaphore_signal(barrier, inc=1, device_id=(g, b, t + 1), device_id_type=MESH)
 
+    if helped:
+        pl.semaphore_signal(barrier, inc=1, device_id=(1 - g, b, t), device_id_type=MESH)
     ends = jnp.where(t == 0, 1, 0) + jnp.where(t == nt - 1, 1, 0)
-    pl.semaphore_wait(barrier, nb + 1 - ends)
+    pl.semaphore_wait(barrier, nb + 1 - ends + (1 if helped else 0))
 
     def remote(src, dst, s, r, device):
         return pltpu.make_async_remote_copy(
@@ -68,26 +77,69 @@
         w_pair(0, i, w_ref.at[i], b).start()
         pltpu.make_async_copy(w_ref.at[i], w_slab(b, i), wl_s.at[i]).start()
 
+    half = kb // 2
+
+    def h_slab(i, c, part):
+        return wh.at[i, pl.ds(pl.multiple_of(c * kb + part * half, 16), half)]
+
+    def h_line(i):
+        src = w_ref.at[i, pl.ds(pl.multiple_of(g * half, 16), half)]
+        return remote(src, h_slab(i, core, g), hz_s.at[i], hz_r.at[i], (g, b, t - sgn))
+
+    def h_group(i, part):
+        slab = h_slab(i, core, part)
+        return remote(slab, slab, hy_s.at[i], hy_r.at[i], (1 - g, b, t))
+
+    def h_pair(i, k, c, part):
+        slab = h_slab(i, c, part)
+        return remote(slab, slab, hp_s.at[k, i], hp_r.at[k, i], partner)
+
+    if helped:
+
+        @pl.when(is_end)
+        def _():
+            for i in range(3):
+                h_line(i).start()
+
     def x_slab(o, c):
         return xg.at[pl.ds(pl.multiple_of(o * rows + c * CHUNK, 16), CHUNK)]
 
-    def up(s, c):
-        slab = x_slab(t - s, c)
+    def x_half(o, c):
+        return xg.at[
+            pl.ds(pl.multiple_of(o * rows + c * CHUNK, 16), CHUNK), pl.ds(pl.multiple_of((1 - chip) * kc, 128), kc)
+        ]
+
+    def up(s, c, slab=x_slab):
+        slab = slab(t - s, c)
         return remote(slab, slab, up_s.at[s, c], up_r.at[s, c], (g, b, t + 1))
 
-    def down(s, c):
-        slab = x_slab(t + s, c)
+    def down(s, c, slab=x_slab):
+        slab = slab(t + s, c)
         return remote(slab, slab, dn_s.at[s, c], dn_r.at[s, c], (g, b, t - 1))
 
-    def from_left(s, c):
-        slab = x_slab(t - s, c)
+    def from_left(s, c, slab=x_slab):
+        slab = slab(t - s, c)
         return remote(slab, slab, up_s.at[s - 1, c], up_r.at[s - 1, c], (g, b, t + 1))
 
-    def from_right(s, c):
-        slab = x_slab(t + s, c)
+    def from_right(s, c, slab=x_slab):
+        slab = slab(t + s, c)
         return remote(slab, slab, dn_s.at[s - 1, c], dn_r.at[s - 1, c], (g, b, t - 1))
 
+    def by_width(narrow, act):
+        if not helped:
+            act(x_slab)
+            return
+
+        @pl.when(narrow)
+        def _():
+            act(x_half)
+
+        @pl.when(jnp.logical_not(narrow))
+        def _():
+            act(x_slab)
+
     gain = 1.0 + scale_ref[...]
+    tokens_copy.wait()
 
     def norm(c, carry):
         x = tokens_ref[pl.ds(pl.multiple_of(c * CHUNK, 16), CHUNK), :].astype(jnp.float32)
@@ -119,27 +171,70 @@
     def _():
         qkvx[1:3, MARGIN + total : 2 * MARGIN + total, :] = zeros
 
-    def relay(s):
-        def body(c, carry):
-            @pl.when(t - s >= 0)
-            def _():
-                from_left(s, c).wait_recv()
+    def relay_left(s):
+        @pl.when(t - s >= 0)
+        def _():
+            def body(c, carry):
+                by_width(jnp.logical_and(t == nt - 1, s >= 2), lambda slab: from_left(s, c, slab).wait_recv())
 
                 @pl.when(t < nt - 1)
                 def _():
-                    up(s, c).start()
-
-            @pl.when(t + s < nt)
-            def _():
-                from_right(s, c).wait_recv()
+                    by_width(t == nt - 2, lambda slab: up(s, c, slab).start())
+
+                return carry
+
+            lax.fori_loop(0, nc, body, 0)
+
+    def relay_right(s):
+        @pl.when(t + s < nt)
+        def _():
+            def body(c, carry):
+                by_width(jnp.logical_and(t == 0, s >= 2), lambda slab: from_right(s, c, slab).wait_recv())
 
                 @pl.when(t > 0)
                 def _():
-                    down(s, c).start()
-
+                    by_width(t == 1, lambda slab: down(s, c, slab).start())
+
+                return carry
+
+            lax.fori_loop(0, nc, body, 0)
+
+    def relay(s):
+        relay_left(s)
+        relay_right(s)
+
+    def relay_far(s):
+        @pl.when(lower)
+        def _():
+            relay_right(s)
+
+        @pl.when(jnp.logical_not(lower))
+        def _():
+            relay_left(s)
+
+    def relay_near(s):
+        @pl.when(lower)
+        def _():
+            relay_left(s)
+
+        @pl.when(jnp.logical_not(lower))
+        def _():
+            relay_right(s)
+
+    def part_send(k):
+        return remote(part_out.at[k], part_in.at[k], pt_s.at[k], pt_r.at[k], (g, b, t + sgn))
+
+    def help_end(k):
+        o = t - sgn * (k + 1)
+        x = xg[pl.ds(pl.multiple_of(o * rows, 16), rows), pl.ds(pl.multiple_of(chip * kc, 128), kc)]
+
+        def one(i, carry):
+            y = jnp.dot(x, wh[i], preferred_element_type=jnp.float32)
+            part_out[k, i] = y.astype(jnp.bfloat16)
             return carry
 
-        lax.fori_loop(0, nc, body, 0)
+        lax.fori_loop(0, 3, one, 0)
+        part_send(k).start()
 
     def halo_up(o):
         return remote(
@@ -155,16 +250,44 @@
             hd_s.at[o], hd_r.at[o], (g, b - 1, t),
         )
 
-    def project(o):
+    def store(i, o, y):
+        qkvx[i, pl.ds(pl.multiple_of(MARGIN + o * rows, 16), rows), :] = y.astype(jnp.bfloat16)
+
+    def whole(o):
         x = xg[pl.ds(pl.multiple_of(o * rows, 16), rows), :]
 
         def one(i, carry):
-            y = jnp.dot(x, wfull[i], preferred_element_type=jnp.float32)
-            qkvx[i, pl.ds(pl.multiple_of(MARGIN + o * rows, 16), rows), :] = y.astype(jnp.bfloat16)
+            store(i, o, jnp.dot(x, wfull[i], preferred_element_type=jnp.float32))
             return carry
 
         lax.fori_loop(0, 3, one, 0)
 
+    def rest(o, k):
+        other = pl.ds(pl.multiple_of((1 - chip) * kc, 128), kc)
+        x = xg[pl.ds(pl.multiple_of(o * rows, 16), rows), other]
+        part_send(k).wait_recv()
+
+        def one(i, carry):
+            y = jnp.dot(x, wfull[i, other, :], preferred_element_type=jnp.float32)
+            store(i, o, y + part_in[k, i].astype(jnp.float32))
+            return carry
+
+        lax.fori_loop(0, 3, one, 0)
+
+    def project(o, s):
+        if helped:
+            narrow = jnp.logical_and(is_end, s >= 2)
+
+            @pl.when(narrow)
+            def _():
+                rest(o, s - 2)
+
+            @pl.when(jnp.logical_not(narrow))
+            def _():
+                whole(o)
+        else:
+            whole(o)
+
         @pl.when(jnp.logical_and(o * rows >= total - MARGIN, b < nb - 1))
         def _():
             halo_up(o).start()
@@ -173,23 +296,56 @@
         def _():
             halo_down(o).start()
 
-    relay(1)
+    if helped:
+        relay_far(1)
+
+        @pl.when(jnp.logical_not(is_end))
+        def _():
+            for i in range(3):
+                h_line(i).wait_recv()
+                h_group(i, g).start()
+                h_pair(i, 0, core, g).start()
+
+        relay_near(1)
+    else:
+        relay(1)
 
     for i in range(3):
         for j in range(1, chips):
             owner = ((chip - j + chips) % chips) * 2 + core
             w_cross(j, i, owner, partner).wait_recv()
             w_pair(j, i, w_slab(owner, i), owner).start()
+
+    if helped:
+
+        @pl.when(jnp.logical_not(is_end))
+        def _():
+            for i in range(3):
+                h_group(i, 1 - g).wait_recv()
+                h_pair(i, 1, core, 1 - g).start()
+
+        relay_far(2)
+
+        @pl.when(jnp.logical_not(is_end))
+        def _():
+            for i in range(3):
+                h_pair(i, 0, 1 - core, g).wait_recv()
+                h_pair(i, 1, 1 - core, 1 - g).wait_recv()
+
+            def assist(k, carry):
+                help_end(k)
+                return carry
+
+            lax.fori_loop(0, nt - 2, assist, 0)
+
     for i in range(3):
         pltpu.make_async_copy(w_ref.at[i], w_slab(b, i), wl_s.at[i]).wait()
         for j in range(chips):
             owner = ((chip - j + chips) % chips) * 2 + (1 - core)
             w_pair(j, i, w_slab(owner, i), owner).wait_recv()
 
-    project(t)
-
     def step(s, carry):
-        @pl.when(s > 1)
+        @pl.when(s > (2 if helped else 1))
         def _():
             relay(s)
 
@@ -198,24 +354,24 @@
 
             @pl.when(jnp.logical_and(o >= 0, o < nt))
             def _():
-                project(o)
+                project(o, s)
 
             return carry
 
-        lax.fori_loop(0, 2, side, 0)
+        lax.fori_loop(jnp.where(s == 0, 1, 0), 2, side, 0)
         return carry
 
-    lax.fori_loop(1, nt, step, 0)
+    lax.fori_loop(0, nt, step, 0)
 
     def drain(s, carry):
         def body(c, carry):
             @pl.when(jnp.logical_and(t - s >= 0, t < nt - 1))
             def _():
-                up(s, c).wait_send()
+                by_width(jnp.logical_and(t == nt - 2, s >= 1), lambda slab: up(s, c, slab).wait_send())
 
             @pl.when(jnp.logical_and(t + s < nt, t > 0))
             def _():
-                down(s, c).wait_send()
+                by_width(jnp.logical_and(t == 1, s >= 1), lambda slab: down(s, c, slab).wait_send())
 
             return carry
 
@@ -227,6 +383,22 @@
             w_cross(j, i, b, partner).wait_send()
         for j in range(chips):
             w_pair(j, i, w_ref.at[i], b).wait_send()
+
+    if helped:
+
+        @pl.when(is_end)
+        def _():
+            for i in range(3):
+                h_line(i).wait_send()
+
+        @pl.when(jnp.logical_not(is_end))
+        def _():
+            for i in range(3):
+                h_group(i, g).wait_send()
+                h_pair(i, 0, core, g).wait_send()
+                h_pair(i, 1, core, 1 - g).wait_send()
+            for k in range(nt - 2):
+                part_send(k).wait_send()
 
     q_ref[...] = qkvx[0, MARGIN : MARGIN + total, :]
 
@@ -280,31 +452,40 @@
             out_ref[p * TILE : (p + 1) * TILE, cols] = mixed.astype(jnp.bfloat16)
 
 
-def shards(nb, nt, tokens, mod_shift, mod_scale, w_qkv, tile_list, tile_count):
+def shards(ng, nb, nt, tokens, mod_shift, mod_scale, w_qkv, tile_list, tile_count):
     rows, d = tokens.shape
     width = w_qkv.shape[2]
     total = rows * nt
     nc = rows // CHUNK
     chips = nb // 2
+    kb = w_qkv.shape[1]
+    helped = ng == 2 and chips == 2 and nt == 4 and kb % 64 == 0
+    help_rows = 2 * kb if helped else 16
+    slots = nt - 2 if helped else 1
     vmem = pl.BlockSpec(memory_space=pltpu.VMEM)
     smem = pl.BlockSpec(memory_space=pltpu.SMEM)
     dma = pltpu.SemaphoreType.DMA
     bf16 = jnp.bfloat16
     q, kv = pl.pallas_call(
-        functools.partial(project_kernel, nb, nt),
+        functools.partial(project_kernel, helped, nb, nt),
         out_shape=(
             jax.ShapeDtypeStruct((total, width), bf16),
             jax.ShapeDtypeStruct((2, total + 2 * MARGIN, width), bf16),
         ),
-        in_specs=[vmem, vmem, vmem, pl.BlockSpec(memory_space=pl.ANY)],
+        in_specs=[pl.BlockSpec(memory_space=pl.ANY), vmem, vmem, pl.BlockSpec(memory_space=pl.ANY)],
         out_specs=(vmem, vmem),
         scratch_shapes=[
+            pltpu.VMEM((rows, d), bf16),
             pltpu.VMEM((total, d), bf16),
             pltpu.VMEM((3, d, width), bf16),
             pltpu.VMEM((3, total + 2 * MARGIN, width), bf16),
+            pltpu.VMEM((3, help_rows, width), bf16),
+            pltpu.VMEM((slots, 3, rows, width), bf16),
+            pltpu.VMEM((slots, 3, rows, width), bf16),
             dma((nt, nc)), dma((nt, nc)), dma((nt, nc)), dma((nt, nc)),
             dma((chips, 3)), dma((chips, 3)), dma((chips, 3)), dma((chips, 3)), dma((3,)),
             dma((nt,)), dma((nt,)), dma((nt,)), dma((nt,)),
+            dma((3,)), dma((3,)), dma((3,)), dma((3,)), dma((2, 3)), dma((2, 3)), dma((slots,)), dma((slots,)), dma,
         ],
         compiler_params=pltpu.CompilerParams(
             collective_id=0, has_side_effects=True, vmem_limit_bytes=40 * 2**20
@@ -321,7 +502,7 @@
 
 def solution(mesh):
     return jax.shard_map(
-        functools.partial(shards, mesh.shape["block"], mesh.shape["tensor"]),
+        functools.partial(shards, mesh.shape["groups"], mesh.shape["block"], mesh.shape["tensor"]),
         mesh=mesh,
         in_specs=(
             P(("groups", "block", "tensor"), None),

time: 104 us -> 94.2 us (0.906)
  Pallas kernels: 99 us -> 89.4 us
    pallas_call x1, Pallas kernels: 94.5 us -> 84.8 us  [shards(): pl.pallas_call(functools.partial(project_kernel, helped, nb, nt), out_sha...]
where the time goes in v2:
time: 94.2 us; the launch traced here: 93.8 us
  Pallas kernels  89.4 us (95%)
  local copies, waits for them, and re-layouts  4.35 us (5%)
    pallas_call x1, Pallas kernels, shards(): pl.pallas_call(functools.partial(project_kernel, helped, nb, nt), out_sha...  84.8 us
    pallas_call x1, Pallas kernels, shards(): pl.pallas_call(attend_kernel, out_shape=jax.ShapeDtypeStruct((total, widt...  4.58 us
    unnamed x12, local copies, waits for them, and re-layouts  4.35 us

profile of v2, /device:TPU:1, one launch (start us, length us, event | category | flops | bytes accessed | tf_op | source)
XLA Modules:
  0.0 93.8 jit_solution(2710261578925268591)
XLA Ops:
  0.0 0.0 copy-start.5
  0.0 0.0 copy-start.4
  0.0 0.0 copy-start
  0.0 1.6 %copy-done = bf16[3,1280,256]{2,1,0:T(8,128)(2,1)S(1)} copy-done((bf16[3,1280,256]{2,1,0:T(8,128)(2,1)S(1)}, bf16[3,1280,256]{2,1,0:T(8,128)(2,1)}, u32[]{:S(2)}) %copy-start) | copy-done | bytes 1966104
  1.6 0.0 copy-start.1
  1.6 1.3 %copy-done.1 = bf16[128,5120]{1,0:T(8,128)(2,1)S(1)} copy-done((bf16[128,5120]{1,0:T(8,128)(2,1)S(1)}, bf16[128,5120]{1,0:T(8,128)(2,1)}, u32[]{:S(2)}) %copy-start.1) | copy-done | bytes 1310744
  2.9 0.0 copy-start.2
  2.9 0.7 copy-done.2
  3.6 0.0 copy-start.3
  3.6 0.7 copy-done.3
  4.4 84.8 %shard_map.64 = (bf16[512,256]{1,0:T(8,128)(2,1)S(1)}, bf16[2,1024,256]{2,1,0:T(8,128)(2,1)S(1)}) custom-call(bf16[128,5120]{1,0:T(8,128)(2,1)S(1)} %copy-done.1, f32[1,5120]{1,0:T(1,128)S(1)} %bitcast.2, f32[1,5120]{1,0:T(1,128)S(1)} %bitcast.3, bf16[3,1280,256]{2,1,0:T(8,128)(2,1)S(1)} %copy-done), custom_call_target="tpu_custom_call" | custom-call | tf_op jit(solution)/shard_map/pallas_call | solution.py:469
  89.2 0.0 copy-done.5
  89.2 0.0 copy-done.4
  89.2 4.6 %shard_map.65 = bf16[512,256]{1,0:T(8,128)(2,1)} custom-call(s32[1,4,5]{2,1,0:T(4,128)S(1)} %copy-done.4, s32[1,4]{1,0:T(1,128)S(1)} %copy-done.5, bf16[512,256]{1,0:T(8,128)(2,1)S(1)} %get-tuple-element.7.q_ref, bf16[2,1024,256]{2,1,0:T(8,128)(2,1)S(1)} %get-tuple-element.8.kv_ref), custom_call_target="tpu_custom_call" | custom-call | tf_op jit(solution)/shard_map/pallas_call | solution.py:494
Async XLA Ops:
  0.0 89.2 %copy-start.5 = (s32[1,4]{1,0:T(1,128)S(1)}, s32[1,4]{1,0:T(1,128)}, u32[]{:S(2)}) copy-start(s32[1,4]{1,0:T(1,128)} %count_ref.1) | copy-start | bytes 52
  0.0 89.2 %copy-start.4 = (s32[1,4,5]{2,1,0:T(4,128)S(1)}, s32[1,4,5]{2,1,0:T(4,128)}, u32[]{:S(2)}) copy-start(s32[1,4,5]{2,1,0:T(4,128)} %list_ref.1) | copy-start | bytes 244
  0.0 1.6 %copy-start = (bf16[3,1280,256]{2,1,0:T(8,128)(2,1)S(1)}, bf16[3,1280,256]{2,1,0:T(8,128)(2,1)}, u32[]{:S(2)}) copy-start(bf16[3,1280,256]{2,1,0:T(8,128)(2,1)} %w_ref.1) | copy-start | bytes 5898244
  1.6 1.3 %copy-start.1 = (bf16[128,5120]{1,0:T(8,128)(2,1)S(1)}, bf16[128,5120]{1,0:T(8,128)(2,1)}, u32[]{:S(2)}) copy-start(bf16[128,5120]{1,0:T(8,128)(2,1)} %tokens_hbm.1) | copy-start | bytes 3932164
  2.9 0.7 copy-start.2
  3.6 0.7 copy-start.3

commit v3 on v2

--- a/solution.py
+++ b/solution.py
@@ -18,12 +18,16 @@
 
 
 def project_kernel(
-    helped, nb, nt, tokens_hbm, shift_ref, scale_ref, w_ref, q_ref, kv_ref,
-    tokens_ref, xg, wfull, qkvx, wh, part_out, part_in, up_s, up_r, dn_s, dn_r, wx_s, wx_r, wp_s, wp_r, wl_s,
-    hu_s, hu_r, hd_s, hd_r, hz_s, hz_r, hy_s, hy_r, hp_s, hp_r, pt_s, pt_r, tk_s,
+    helped, nb, nt, tokens_hbm, shift_hbm, scale_hbm, w_ref, q_ref, kv_ref,
+    tokens_ref, shift_ref, scale_ref, xg, wfull, qkvx, wh, part_out, part_in, up_s, up_r, dn_s, dn_r, wx_s, wx_r, wp_s, wp_r, wl_s,
+    hu_s, hu_r, hd_s, hd_r, hz_s, hz_r, hy_s, hy_r, hp_s, hp_r, pt_s, pt_r, tk_s, sh_s, sc_s,
 ):
     tokens_copy = pltpu.make_async_copy(tokens_hbm, tokens_ref, tk_s)
     tokens_copy.start()
+    shift_copy = pltpu.make_async_copy(shift_hbm, shift_ref, sh_s)
+    shift_copy.start()
+    scale_copy = pltpu.make_async_copy(scale_hbm, scale_ref, sc_s)
+    scale_copy.start()
     g = lax.axis_index("groups")
     b = lax.axis_index("block")
     t = lax.axis_index("tensor")
@@ -138,8 +142,10 @@
         def _():
             act(x_slab)
 
+    scale_copy.wait()
+    shift_copy.wait()
+    tokens_copy.wait()
     gain = 1.0 + scale_ref[...]
-    tokens_copy.wait()
 
     def norm(c, carry):
         x = tokens_ref[pl.ds(pl.multiple_of(c * CHUNK, 16), CHUNK), :].astype(jnp.float32)
@@ -159,6 +165,13 @@
 
         return carry
 
+    if helped:
+
+        @pl.when(is_end)
+        def _():
+            for i in range(3):
+                h_line(i).wait_send()
+
     lax.fori_loop(0, nc, norm, 0)
 
     zeros = jnp.zeros((2, MARGIN, qkvx.shape[2]), qkvx.dtype)
@@ -171,7 +184,7 @@
     def _():
         qkvx[1:3, MARGIN + total : 2 * MARGIN + total, :] = zeros
 
-    def relay_left(s):
+    def relay_left(s, after=None):
         @pl.when(t - s >= 0)
         def _():
             def body(c, carry):
@@ -181,11 +194,13 @@
                 def _():
                     by_width(t == nt - 2, lambda slab: up(s, c, slab).start())
 
+                if after is not None:
+                    after(c)
                 return carry
 
             lax.fori_loop(0, nc, body, 0)
 
-    def relay_right(s):
+    def relay_right(s, after=None):
         @pl.when(t + s < nt)
         def _():
             def body(c, carry):
@@ -195,6 +210,8 @@
                 def _():
                     by_width(t == 1, lambda slab: down(s, c, slab).start())
 
+                if after is not None:
+                    after(c)
                 return carry
 
             lax.fori_loop(0, nc, body, 0)
@@ -203,14 +220,14 @@
         relay_left(s)
         relay_right(s)
 
-    def relay_far(s):
+    def relay_far(s, after=None):
         @pl.when(lower)
         def _():
-            relay_right(s)
+            relay_right(s, after)
 
         @pl.when(jnp.logical_not(lower))
         def _():
-            relay_left(s)
+            relay_left(s, after)
 
     def relay_near(s):
         @pl.when(lower)
@@ -288,6 +305,9 @@
         else:
             whole(o)
 
+        halos(o)
+
+    def halos(o):
         @pl.when(jnp.logical_and(o * rows >= total - MARGIN, b < nb - 1))
         def _():
             halo_up(o).start()
@@ -297,7 +317,6 @@
             halo_down(o).start()
 
     if helped:
-        relay_far(1)
 
         @pl.when(jnp.logical_not(is_end))
         def _():
@@ -306,6 +325,7 @@
                 h_group(i, g).start()
                 h_pair(i, 0, core, g).start()
 
+        relay_far(1)
         relay_near(1)
     else:
         relay(1)
@@ -324,26 +344,45 @@
                 h_group(i, 1 - g).wait_recv()
                 h_pair(i, 1, core, 1 - g).start()
 
-        relay_far(2)
-
-        @pl.when(jnp.logical_not(is_end))
-        def _():
-            for i in range(3):
-                h_pair(i, 0, 1 - core, g).wait_recv()
-                h_pair(i, 1, 1 - core, 1 - g).wait_recv()
-
-            def assist(k, carry):
-                help_end(k)
-                return carry
-
-            lax.fori_loop(0, nt - 2, assist, 0)
-
     for i in range(3):
         pltpu.make_async_copy(w_ref.at[i], w_slab(b, i), wl_s.at[i]).wait()
         for j in range(chips):
             owner = ((chip - j + chips) % chips) * 2 + (1 - core)
             w_pair(j, i, w_slab(owner, i), owner).wait_recv()
 
+    if helped:
+        each = -(-6 // nc)
+
+        def between(c):
+            def unit(u, carry):
+                o = t - sgn * (u // 3)
+                i = u % 3
+                x = xg[pl.ds(pl.multiple_of(o * rows, 16), rows), :]
+                store(i, o, jnp.dot(x, wfull[i], preferred_element_type=jnp.float32))
+                return carry
+
+            lax.fori_loop(jnp.minimum(each * c, 6), jnp.minimum(each * (c + 1), 6), unit, 0)
+
+            @pl.when(jnp.logical_and(c == min(1, nc - 1), jnp.logical_not(is_end)))
+            def _():
+                for i in range(3):
+                    h_pair(i, 0, 1 - core, g).wait_recv()
+                    h_pair(i, 1, 1 - core, 1 - g).wait_recv()
+                help_end(0)
+
+        relay_far(2, between)
+
+        @pl.when(jnp.logical_not(is_end))
+        def _():
+            def assist(k, carry):
+                help_end(k)
+                return carry
+
+            lax.fori_loop(1, nt - 2, assist, 0)
+
+        halos(t)
+        halos(t - sgn)
+
     def step(s, carry):
         @pl.when(s > (2 if helped else 1))
         def _():
@@ -351,8 +390,11 @@
 
         def side(d, carry):
             o = t + s * (2 * d - 1)
-
-            @pl.when(jnp.logical_and(o >= 0, o < nt))
+            todo = jnp.logical_and(o >= 0, o < nt)
+            if helped:
+                todo = jnp.logical_and(todo, o != t - sgn)
+
+            @pl.when(todo)
             def _():
                 project(o, s)
 
@@ -361,7 +403,7 @@
         lax.fori_loop(jnp.where(s == 0, 1, 0), 2, side, 0)
         return carry
 
-    lax.fori_loop(0, nt, step, 0)
+    lax.fori_loop(1 if helped else 0, nt, step, 0)
 
     def drain(s, carry):
         def body(c, carry):
@@ -385,11 +427,6 @@
             w_pair(j, i, w_ref.at[i], b).wait_send()
 
     if helped:
-
-        @pl.when(is_end)
-        def _():
-            for i in range(3):
-                h_line(i).wait_send()
 
         @pl.when(jnp.logical_not(is_end))
         def _():
@@ -472,10 +509,12 @@
             jax.ShapeDtypeStruct((total, width), bf16),
             jax.ShapeDtypeStruct((2, total + 2 * MARGIN, width), bf16),
         ),
-        in_specs=[pl.BlockSpec(memory_space=pl.ANY), vmem, vmem, pl.BlockSpec(memory_space=pl.ANY)],
+        in_specs=[pl.BlockSpec(memory_space=pl.ANY)] * 4,
         out_specs=(vmem, vmem),
         scratch_shapes=[
             pltpu.VMEM((rows, d), bf16),
+            pltpu.VMEM((1, d), jnp.float32),
+            pltpu.VMEM((1, d), jnp.float32),
             pltpu.VMEM((total, d), bf16),
             pltpu.VMEM((3, d, width), bf16),
             pltpu.VMEM((3, total + 2 * MARGIN, width), bf16),
@@ -485,7 +524,7 @@
             dma((nt, nc)), dma((nt, nc)), dma((nt, nc)), dma((nt, nc)),
             dma((chips, 3)), dma((chips, 3)), dma((chips, 3)), dma((chips, 3)), dma((3,)),
             dma((nt,)), dma((nt,)), dma((nt,)), dma((nt,)),
-            dma((3,)), dma((3,)), dma((3,)), dma((3,)), dma((2, 3)), dma((2, 3)), dma((slots,)), dma((slots,)), dma,
+            dma((3,)), dma((3,)), dma((3,)), dma((3,)), dma((2, 3)), dma((2, 3)), dma((slots,)), dma((slots,)), dma, dma, dma,
         ],
         compiler_params=pltpu.CompilerParams(
             collective_id=0, has_side_effects=True, vmem_limit_bytes=40 * 2**20

time: 94.2 us -> 95.9 us (1.018)
  Pallas kernels: 89.4 us -> 91 us
    pallas_call x1, Pallas kernels: 84.8 us -> 86.4 us  [shards(): pl.pallas_call(functools.partial(project_kernel, helped, nb, nt), out_sha...]
where the time goes in v3:
time: 95.9 us; the launch traced here: 95.4 us
  Pallas kernels  91 us (95%)
  local copies, waits for them, and re-layouts  4.35 us (5%)
    pallas_call x1, Pallas kernels, shards(): pl.pallas_call(functools.partial(project_kernel, helped, nb, nt), out_sha...  86.4 us
    pallas_call x1, Pallas kernels, shards(): pl.pallas_call(attend_kernel, out_shape=jax.ShapeDtypeStruct((total, widt...  4.58 us
    unnamed x12, local copies, waits for them, and re-layouts  4.35 us

profile of v3, /device:TPU:1, one launch (start us, length us, event | category | flops | bytes accessed | tf_op | source)
XLA Modules:
  0.0 95.4 jit_solution(11418870965654213369)
XLA Ops:
  0.0 0.0 copy-start.5
  0.0 0.0 copy-start.4
  0.0 0.0 copy-start
  0.0 1.6 %copy-done = bf16[3,1280,256]{2,1,0:T(8,128)(2,1)S(1)} copy-done((bf16[3,1280,256]{2,1,0:T(8,128)(2,1)S(1)}, bf16[3,1280,256]{2,1,0:T(8,128)(2,1)}, u32[]{:S(2)}) %copy-start) | copy-done | bytes 1966104
  1.6 0.0 copy-start.1
  1.6 1.3 %copy-done.1 = bf16[128,5120]{1,0:T(8,128)(2,1)S(1)} copy-done((bf16[128,5120]{1,0:T(8,128)(2,1)S(1)}, bf16[128,5120]{1,0:T(8,128)(2,1)}, u32[]{:S(2)}) %copy-start.1) | copy-done | bytes 1310744
  2.9 0.0 copy-start.2
  2.9 0.7 copy-done.2
  3.6 0.0 copy-start.3
  3.6 0.7 copy-done.3
  4.4 86.4 %shard_map.64 = (bf16[512,256]{1,0:T(8,128)(2,1)S(1)}, bf16[2,1024,256]{2,1,0:T(8,128)(2,1)S(1)}) custom-call(bf16[128,5120]{1,0:T(8,128)(2,1)S(1)} %copy-done.1, f32[1,5120]{1,0:T(1,128)S(1)} %bitcast.2, f32[1,5120]{1,0:T(1,128)S(1)} %bitcast.3, bf16[3,1280,256]{2,1,0:T(8,128)(2,1)S(1)} %copy-done), custom_call_target="tpu_custom_call" | custom-call | tf_op jit(solution)/shard_map/pallas_call | solution.py:506
  90.8 0.0 copy-done.5
  90.8 0.0 copy-done.4
  90.8 4.6 %shard_map.65 = bf16[512,256]{1,0:T(8,128)(2,1)} custom-call(s32[1,4,5]{2,1,0:T(4,128)S(1)} %copy-done.4, s32[1,4]{1,0:T(1,128)S(1)} %copy-done.5, bf16[512,256]{1,0:T(8,128)(2,1)S(1)} %get-tuple-element.7.q_ref, bf16[2,1024,256]{2,1,0:T(8,128)(2,1)S(1)} %get-tuple-element.8.kv_ref), custom_call_target="tpu_custom_call" | custom-call | tf_op jit(solution)/shard_map/pallas_call | solution.py:533
Async XLA Ops:
  0.0 90.8 %copy-start.5 = (s32[1,4]{1,0:T(1,128)S(1)}, s32[1,4]{1,0:T(1,128)}, u32[]{:S(2)}) copy-start(s32[1,4]{1,0:T(1,128)} %count_ref.1) | copy-start | bytes 52
  0.0 90.8 %copy-start.4 = (s32[1,4,5]{2,1,0:T(4,128)S(1)}, s32[1,4,5]{2,1,0:T(4,128)}, u32[]{:S(2)}) copy-start(s32[1,4,5]{2,1,0:T(4,128)} %list_ref.1) | copy-start | bytes 244
  0.0 1.6 %copy-start = (bf16[3,1280,256]{2,1,0:T(8,128)(2,1)S(1)}, bf16[3,1280,256]{2,1,0:T(8,128)(2,1)}, u32[]{:S(2)}) copy-start(bf16[3,1280,256]{2,1,0:T(8,128)(2,1)} %w_ref.1) | copy-start | bytes 5898244
  1.6 1.3 %copy-start.1 = (bf16[128,5120]{1,0:T(8,128)(2,1)S(1)}, bf16[128,5120]{1,0:T(8,128)(2,1)}, u32[]{:S(2)}) copy-start(bf16[128,5120]{1,0:T(8,128)(2,1)} %tokens_hbm.1) | copy-start | bytes 3932164
  2.9 0.7 copy-start.2
  3.6 0.7 copy-start.3

commit v4 on v3

--- a/solution.py
+++ b/solution.py
@@ -98,13 +98,6 @@
         slab = h_slab(i, c, part)
         return remote(slab, slab, hp_s.at[k, i], hp_r.at[k, i], partner)
 
-    if helped:
-
-        @pl.when(is_end)
-        def _():
-            for i in range(3):
-                h_line(i).start()
-
     def x_slab(o, c):
         return xg.at[pl.ds(pl.multiple_of(o * rows + c * CHUNK, 16), CHUNK)]
 
@@ -165,14 +158,14 @@
 
         return carry
 
+    lax.fori_loop(0, nc, norm, 0)
     if helped:
 
         @pl.when(is_end)
         def _():
             for i in range(3):
-                h_line(i).wait_send()
-
-    lax.fori_loop(0, nc, norm, 0)
+                h_line(i).start()
+
 
     zeros = jnp.zeros((2, MARGIN, qkvx.shape[2]), qkvx.dtype)
 
@@ -317,14 +310,6 @@
             halo_down(o).start()
 
     if helped:
-
-        @pl.when(jnp.logical_not(is_end))
-        def _():
-            for i in range(3):
-                h_line(i).wait_recv()
-                h_group(i, g).start()
-                h_pair(i, 0, core, g).start()
-
         relay_far(1)
         relay_near(1)
     else:
@@ -341,8 +326,9 @@
         @pl.when(jnp.logical_not(is_end))
         def _():
             for i in range(3):
-                h_group(i, 1 - g).wait_recv()
-                h_pair(i, 1, core, 1 - g).start()
+                h_line(i).wait_recv()
+                h_group(i, g).start()
+                h_pair(i, 0, core, g).start()
 
     for i in range(3):
         pltpu.make_async_copy(w_ref.at[i], w_slab(b, i), wl_s.at[i]).wait()
@@ -363,22 +349,22 @@
 
             lax.fori_loop(jnp.minimum(each * c, 6), jnp.minimum(each * (c + 1), 6), unit, 0)
 
-            @pl.when(jnp.logical_and(c == min(1, nc - 1), jnp.logical_not(is_end)))
-            def _():
-                for i in range(3):
-                    h_pair(i, 0, 1 - core, g).wait_recv()
-                    h_pair(i, 1, 1 - core, 1 - g).wait_recv()
-                help_end(0)
-
         relay_far(2, between)
 
         @pl.when(jnp.logical_not(is_end))
         def _():
+            for i in range(3):
+                h_group(i, 1 - g).wait_recv()
+                h_pair(i, 1, core, 1 - g).start()
+            for i in range(3):
+                h_pair(i, 0, 1 - core, g).wait_recv()
+                h_pair(i, 1, 1 - core, 1 - g).wait_recv()
+
             def assist(k, carry):
                 help_end(k)
                 return carry
 
-            lax.fori_loop(1, nt - 2, assist, 0)
+            lax.fori_loop(0, nt - 2, assist, 0)
 
         halos(t)
         halos(t - sgn)
@@ -427,6 +413,11 @@
             w_pair(j, i, w_ref.at[i], b).wait_send()
 
     if helped:
+
+        @pl.when(is_end)
+        def _():
+            for i in range(3):
+                h_line(i).wait_send()
 
         @pl.when(jnp.logical_not(is_end))
         def _():
@@ -527,7 +518,7 @@
             dma((3,)), dma((3,)), dma((3,)), dma((3,)), dma((2, 3)), dma((2, 3)), dma((slots,)), dma((slots,)), dma, dma, dma,
         ],
         compiler_params=pltpu.CompilerParams(
-            collective_id=0, has_side_effects=True, vmem_limit_bytes=40 * 2**20
+            collective_id=0, has_side_effects=True, vmem_limit_bytes=60 * 2**20
         ),
     )(tokens, mod_shift.reshape(1, d), mod_scale.reshape(1, d), w_qkv)
     return pl.pallas_call(

time: 95.9 us -> 94 us (0.980)
  local copies, waits for them, and re-layouts: 4.35 us -> 2.17 us
    unnamed x12 -> x8, local copies, waits for them, and re-layouts: 4.35 us -> 2.17 us
where the time goes in v4:
time: 94 us; the launch traced here: 93.8 us
  Pallas kernels  91.6 us (97%)
  local copies, waits for them, and re-layouts  2.17 us (2%)
    pallas_call x1, Pallas kernels, shards(): pl.pallas_call(functools.partial(project_kernel, helped, nb, nt), out_sha...  87.1 us
    pallas_call x1, Pallas kernels, shards(): pl.pallas_call(attend_kernel, out_shape=jax.ShapeDtypeStruct((total, widt...  4.55 us
    unnamed x8, local copies, waits for them, and re-layouts  2.17 us

profile of v4, /device:TPU:1, one launch (start us, length us, event | category | flops | bytes accessed | tf_op | source)
XLA Modules:
  0.0 93.8 jit_solution(15637441010614644240)
XLA Ops:
  0.0 0.0 copy-start.3
  0.0 0.0 copy-start.2
  0.0 87.1 %shard_map.64 = (bf16[512,256]{1,0:T(8,128)(2,1)}, bf16[2,1024,256]{2,1,0:T(8,128)(2,1)}) custom-call(bf16[128,5120]{1,0:T(8,128)(2,1)} %tokens_hbm.1, f32[1,5120]{1,0:T(1,128)} %bitcast.2, f32[1,5120]{1,0:T(1,128)} %bitcast.3, bf16[3,1280,256]{2,1,0:T(8,128)(2,1)} %w_ref.1), custom_call_target="tpu_custom_call" | custom-call | tf_op jit(solution)/shard_map/pallas_call | solution.py:497
  87.1 0.0 copy-done.3
  87.1 0.0 copy-done.2
  87.1 0.0 copy-start
  87.1 1.2 %copy-done = bf16[2,1024,256]{2,1,0:T(8,128)(2,1)S(1)} copy-done((bf16[2,1024,256]{2,1,0:T(8,128)(2,1)S(1)}, bf16[2,1024,256]{2,1,0:T(8,128)(2,1)}, u32[]{:S(2)}) %copy-start) | copy-done | bytes 1048600
  88.3 0.0 copy-start.1
  88.3 0.9 %copy-done.1 = bf16[512,256]{1,0:T(8,128)(2,1)S(1)} copy-done((bf16[512,256]{1,0:T(8,128)(2,1)S(1)}, bf16[512,256]{1,0:T(8,128)(2,1)}, u32[]{:S(2)}) %copy-start.1) | copy-done | bytes 262168
  89.3 4.5 %shard_map.65 = bf16[512,256]{1,0:T(8,128)(2,1)} custom-call(s32[1,4,5]{2,1,0:T(4,128)S(1)} %copy-done.2, s32[1,4]{1,0:T(1,128)S(1)} %copy-done.3, bf16[512,256]{1,0:T(8,128)(2,1)S(1)} %copy-done.1, bf16[2,1024,256]{2,1,0:T(8,128)(2,1)S(1)} %copy-done), custom_call_target="tpu_custom_call" | custom-call | tf_op jit(solution)/shard_map/pallas_call | solution.py:524
Async XLA Ops:
  0.0 87.1 %copy-start.3 = (s32[1,4]{1,0:T(1,128)S(1)}, s32[1,4]{1,0:T(1,128)}, u32[]{:S(2)}) copy-start(s32[1,4]{1,0:T(1,128)} %count_ref.1) | copy-start | bytes 52
  0.0 87.1 %copy-start.2 = (s32[1,4,5]{2,1,0:T(4,128)S(1)}, s32[1,4,5]{2,1,0:T(4,128)}, u32[]{:S(2)}) copy-start(s32[1,4,5]{2,1,0:T(4,128)} %list_ref.1) | copy-start | bytes 244
  87.1 1.2 %copy-start = (bf16[2,1024,256]{2,1,0:T(8,128)(2,1)S(1)}, bf16[2,1024,256]{2,1,0:T(8,128)(2,1)}, u32[]{:S(2)}) copy-start(bf16[2,1024,256]{2,1,0:T(8,128)(2,1)} %get-tuple-element.8.kv_ref) | copy-start | bytes 3145732
  88.3 0.9 %copy-start.1 = (bf16[512,256]{1,0:T(8,128)(2,1)S(1)}, bf16[512,256]{1,0:T(8,128)(2,1)}, u32[]{:S(2)}) copy-start(bf16[512,256]{1,0:T(8,128)(2,1)} %get-tuple-element.7.q_ref) | copy-start | bytes 786436

commit v5 on v2

--- a/solution.py
+++ b/solution.py
@@ -18,12 +18,16 @@
 
 
 def project_kernel(
-    helped, nb, nt, tokens_hbm, shift_ref, scale_ref, w_ref, q_ref, kv_ref,
-    tokens_ref, xg, wfull, qkvx, wh, part_out, part_in, up_s, up_r, dn_s, dn_r, wx_s, wx_r, wp_s, wp_r, wl_s,
-    hu_s, hu_r, hd_s, hd_r, hz_s, hz_r, hy_s, hy_r, hp_s, hp_r, pt_s, pt_r, tk_s,
+    helped, nb, nt, tokens_hbm, shift_hbm, scale_hbm, w_ref, q_ref, kv_ref,
+    tokens_ref, shift_ref, scale_ref, xg, wfull, qkvx, wh, part_out, part_in, up_s, up_r, dn_s, dn_r, wx_s, wx_r, wp_s, wp_r, wl_s,
+    hu_s, hu_r, hd_s, hd_r, hz_s, hz_r, hy_s, hy_r, hp_s, hp_r, pt_s, pt_r, tk_s, sh_s, sc_s,
 ):
     tokens_copy = pltpu.make_async_copy(tokens_hbm, tokens_ref, tk_s)
     tokens_copy.start()
+    shift_copy = pltpu.make_async_copy(shift_hbm, shift_ref, sh_s)
+    shift_copy.start()
+    scale_copy = pltpu.make_async_copy(scale_hbm, scale_ref, sc_s)
+    scale_copy.start()
     g = lax.axis_index("groups")
     b = lax.axis_index("block")
     t = lax.axis_index("tensor")
@@ -138,8 +142,10 @@
         def _():
             act(x_slab)
 
+    scale_copy.wait()
+    shift_copy.wait()
+    tokens_copy.wait()
     gain = 1.0 + scale_ref[...]
-    tokens_copy.wait()
 
     def norm(c, carry):
         x = tokens_ref[pl.ds(pl.multiple_of(c * CHUNK, 16), CHUNK), :].astype(jnp.float32)
@@ -472,10 +478,12 @@
             jax.ShapeDtypeStruct((total, width), bf16),
             jax.ShapeDtypeStruct((2, total + 2 * MARGIN, width), bf16),
         ),
-        in_specs=[pl.BlockSpec(memory_space=pl.ANY), vmem, vmem, pl.BlockSpec(memory_space=pl.ANY)],
+        in_specs=[pl.BlockSpec(memory_space=pl.ANY)] * 4,
         out_specs=(vmem, vmem),
         scratch_shapes=[
             pltpu.VMEM((rows, d), bf16),
+            pltpu.VMEM((1, d), jnp.float32),
+            pltpu.VMEM((1, d), jnp.float32),
             pltpu.VMEM((total, d), bf16),
             pltpu.VMEM((3, d, width), bf16),
             pltpu.VMEM((3, total + 2 * MARGIN, width), bf16),
@@ -485,10 +493,10 @@
             dma((nt, nc)), dma((nt, nc)), dma((nt, nc)), dma((nt, nc)),
             dma((chips, 3)), dma((chips, 3)), dma((chips, 3)), dma((chips, 3)), dma((3,)),
             dma((nt,)), dma((nt,)), dma((nt,)), dma((nt,)),
-            dma((3,)), dma((3,)), dma((3,)), dma((3,)), dma((2, 3)), dma((2, 3)), dma((slots,)), dma((slots,)), dma,
+            dma((3,)), dma((3,)), dma((3,)), dma((3,)), dma((2, 3)), dma((2, 3)), dma((slots,)), dma((slots,)), dma, dma, dma,
         ],
         compiler_params=pltpu.CompilerParams(
-            collective_id=0, has_side_effects=True, vmem_limit_bytes=40 * 2**20
+            collective_id=0, has_side_effects=True, vmem_limit_bytes=60 * 2**20
         ),
     )(tokens, mod_shift.reshape(1, d), mod_scale.reshape(1, d), w_qkv)
     return pl.pallas_call(

time: 94.2 us -> 92.2 us (0.979)
  local copies, waits for them, and re-layouts: 4.35 us -> 2.17 us
    unnamed x12 -> x8, local copies, waits for them, and re-layouts: 4.35 us -> 2.17 us
where the time goes in v5:
time: 92.2 us; the launch traced here: 91.9 us
  Pallas kernels  89.7 us (97%)
  local copies, waits for them, and re-layouts  2.17 us (2%)
    pallas_call x1, Pallas kernels, shards(): pl.pallas_call(functools.partial(project_kernel, helped, nb, nt), out_sha...  85.2 us
    pallas_call x1, Pallas kernels, shards(): pl.pallas_call(attend_kernel, out_shape=jax.ShapeDtypeStruct((total, widt...  4.55 us
    unnamed x8, local copies, waits for them, and re-layouts  2.17 us

profile of v5, /device:TPU:1, one launch (start us, length us, event | category | flops | bytes accessed | tf_op | source)
XLA Modules:
  0.0 91.9 jit_solution(510991666365164381)
XLA Ops:
  0.0 0.0 copy-start.3
  0.0 0.0 copy-start.2
  0.0 85.2 %shard_map.64 = (bf16[512,256]{1,0:T(8,128)(2,1)}, bf16[2,1024,256]{2,1,0:T(8,128)(2,1)}) custom-call(bf16[128,5120]{1,0:T(8,128)(2,1)} %tokens_hbm.1, f32[1,5120]{1,0:T(1,128)} %bitcast.2, f32[1,5120]{1,0:T(1,128)} %bitcast.3, bf16[3,1280,256]{2,1,0:T(8,128)(2,1)} %w_ref.1), custom_call_target="tpu_custom_call" | custom-call | tf_op jit(solution)/shard_map/pallas_call | solution.py:475
  85.2 0.0 copy-done.3
  85.2 0.0 copy-done.2
  85.2 0.0 copy-start
  85.2 1.2 %copy-done = bf16[2,1024,256]{2,1,0:T(8,128)(2,1)S(1)} copy-done((bf16[2,1024,256]{2,1,0:T(8,128)(2,1)S(1)}, bf16[2,1024,256]{2,1,0:T(8,128)(2,1)}, u32[]{:S(2)}) %copy-start) | copy-done | bytes 1048600
  86.4 0.0 copy-start.1
  86.4 0.9 %copy-done.1 = bf16[512,256]{1,0:T(8,128)(2,1)S(1)} copy-done((bf16[512,256]{1,0:T(8,128)(2,1)S(1)}, bf16[512,256]{1,0:T(8,128)(2,1)}, u32[]{:S(2)}) %copy-start.1) | copy-done | bytes 262168
  87.4 4.5 %shard_map.65 = bf16[512,256]{1,0:T(8,128)(2,1)} custom-call(s32[1,4,5]{2,1,0:T(4,128)S(1)} %copy-done.2, s32[1,4]{1,0:T(1,128)S(1)} %copy-done.3, bf16[512,256]{1,0:T(8,128)(2,1)S(1)} %copy-done.1, bf16[2,1024,256]{2,1,0:T(8,128)(2,1)S(1)} %copy-done), custom_call_target="tpu_custom_call" | custom-call | tf_op jit(solution)/shard_map/pallas_call | solution.py:502
Async XLA Ops:
  0.0 85.2 %copy-start.3 = (s32[1,4]{1,0:T(1,128)S(1)}, s32[1,4]{1,0:T(1,128)}, u32[]{:S(2)}) copy-start(s32[1,4]{1,0:T(1,128)} %count_ref.1) | copy-start | bytes 52
  0.0 85.2 %copy-start.2 = (s32[1,4,5]{2,1,0:T(4,128)S(1)}, s32[1,4,5]{2,1,0:T(4,128)}, u32[]{:S(2)}) copy-start(s32[1,4,5]{2,1,0:T(4,128)} %list_ref.1) | copy-start | bytes 244
  85.2 1.2 %copy-start = (bf16[2,1024,256]{2,1,0:T(8,128)(2,1)S(1)}, bf16[2,1024,256]{2,1,0:T(8,128)(2,1)}, u32[]{:S(2)}) copy-start(bf16[2,1024,256]{2,1,0:T(8,128)(2,1)} %get-tuple-element.8.kv_ref) | copy-start | bytes 3145732
  86.4 0.9 %copy-start.1 = (bf16[512,256]{1,0:T(8,128)(2,1)S(1)}, bf16[512,256]{1,0:T(8,128)(2,1)}, u32[]{:S(2)}) copy-start(bf16[512,256]{1,0:T(8,128)(2,1)} %get-tuple-element.7.q_ref) | copy-start | bytes 786436
